TPU v7x, 32 devices: a whole 2x2x4 slice. The times are simulated.
32 devices in a mesh: seq: 16 (over z, y, x), head: 2 (over core).
Axes of the slice: x: 2, y: 2, z: 4, core: 2. Of those that a mesh axis runs over, the one named last changes fastest.
Arguments:
- q_lin: bfloat16 [4096, 512], P('seq', 'head'), may hold values from -6 to 6
- k_lin: bfloat16 [4096, 512], P('seq', 'head'), may hold values from -6 to 6
- v_lin: bfloat16 [4096, 512], P('seq', 'head'), may hold values from -6 to 6
- log_decay: float32 [4, 4096], P('head', 'seq'), may hold values from -0.4 to 0, as said below
- q_soft: bfloat16 [4096, 512], P('seq', 'head'), may hold values from -12 to 12
- k_soft: bfloat16 [4096, 512], P('seq', 'head'), may hold values from -6 to 6
- v_soft: bfloat16 [4096, 512], P('seq', 'head'), may hold values from -6 to 6
- wo_lin: bfloat16 [512, 4096], P('head'), may hold values from -0.375 to 0.375
- wo_soft: bfloat16 [512, 4096], P('head'), may hold values from -0.375 to 0.375
Outputs:
- lin_mixed: bfloat16 [4096, 4096], P('seq', 'head')
- soft_mixed: bfloat16 [4096, 4096], P('seq', 'head')
Inputs may be any that keep to these rules, and one draw needn't show every extreme that they name: `log_decay`: log decays are never positive.
All inputs are finite; a program needn't handle non-finite values.
Results may differ from a plain program's by a relative error of at most 0.012.
Values may be sent and summed in bfloat16 or wider, within the bound.
A program may use at most 64 MiB of HBM per device.

v0:
```python
import math
import jax
import jax.numpy as jnp
from jax import lax
from jax.sharding import PartitionSpec as P

HIGHEST = lax.Precision.HIGHEST
NEG_BIG = -1e30


def prefix(shard, axis, combine, identity):
    size, here = (lax.axis_size(axis), lax.axis_index(axis))
    everything = jax.tree.map(
        lambda part, kind: lax.all_gather(part.astype(kind), axis),
        shard,
        (jnp.bfloat16, jnp.bfloat16),
    )
    start = jax.tree.map(
        lambda part, zero: jnp.broadcast_to(jnp.asarray(zero, part.dtype), part.shape),
        shard,
        identity,
    )

    def turn(k, before):
        reached = k < here
        new = combine(
            before, jax.tree.map(lambda part, own: part[k].astype(own.dtype), everything, shard)
        )
        return jax.tree.map(lambda a, b: jnp.where(reached, a, b), new, before)

    return lax.fori_loop(0, size, turn, start)


def second_half(device):
    return 2 * device + 1


def absorb(state, query_half, key_block, value_block, allowed, factor):
    row_top, row_sum, weighted = state
    scores = (
        jnp.einsum("qhd,khd->hqk", query_half, key_block, preferred_element_type=jnp.float32)
        * factor
    )
    if allowed is not None:
        scores = jnp.where(allowed[None], scores, -jnp.inf)
    new_top = jnp.maximum(row_top, jnp.max(scores, axis=-1))
    shrink = jnp.exp(row_top - new_top)
    weights = jnp.exp(scores - new_top[:, :, None])
    row_sum = row_sum * shrink + jnp.sum(weights, axis=-1)
    weighted = weighted * shrink.T[:, :, None] + jnp.einsum(
        "hqk,khd->qhd",
        weights.astype(jnp.bfloat16),
        value_block,
        preferred_element_type=jnp.float32,
    )
    return (new_top, row_sum, weighted)


def lightning_heads(q_lin, k_lin, v_lin, log_decay):
    row_count = q_lin.shape[0]
    head_count = log_decay.shape[0]
    head_width = q_lin.shape[1] // head_count
    query_plain = q_lin.reshape(row_count, head_count, head_width)
    key_plain = k_lin.reshape(row_count, head_count, head_width)
    queries = query_plain.astype(jnp.float32)
    key_rows = key_plain.astype(jnp.float32)
    values = v_lin.astype(jnp.float32).reshape(row_count, head_count, head_width)
    cumulative = jnp.cumsum(log_decay, axis=1)
    lower = jnp.arange(row_count)[:, None] >= jnp.arange(row_count)[None, :]
    decay_gap = jnp.where(lower[None], cumulative[:, :, None] - cumulative[:, None, :], -jnp.inf)
    scores = jnp.einsum(
        "thd,shd->hts", query_plain, key_plain, preferred_element_type=jnp.float32
    ) * jnp.exp(decay_gap)
    inside = jnp.einsum("hts,shd->thd", scores, values, precision=HIGHEST)
    closing = jnp.exp(cumulative[:, -1:] - cumulative)
    own_state = jnp.einsum(
        "shd,she->hde", key_rows * closing.T[:, :, None], values, precision=HIGHEST
    )
    own_decay = cumulative[:, -1]

    def combine(earlier, later):
        return (jnp.exp(later[1])[:, None, None] * earlier[0] + later[0], earlier[1] + later[1])

    identity = (jnp.zeros_like(own_state), jnp.zeros_like(own_decay))
    carried, _ = prefix((own_state, own_decay), "seq", combine, identity)
    from_before = (
        jnp.einsum("thd,hde->the", queries, carried, precision=HIGHEST)
        * jnp.exp(cumulative).T[:, :, None]
    )
    raw = inside + from_before
    factor = lax.rsqrt(jnp.mean(raw * raw, axis=-1, keepdims=True) + 1e-06)
    return (raw * factor).astype(jnp.bfloat16).reshape(row_count, head_count * head_width)


def softmax_heads(q_soft, k_soft, v_soft, head_width):
    row_count = q_soft.shape[0]
    half_rows = row_count // 2
    head_count = q_soft.shape[1] // head_width
    own_index = lax.axis_index("seq")
    factor = 1.0 / math.sqrt(head_width)
    shaped = q_soft.reshape(2, half_rows, head_count, head_width)
    query_ids = (2 * own_index, second_half(own_index))
    triangle = jnp.arange(half_rows)[:, None] >= jnp.arange(half_rows)[None, :]

    def block_pass(state, side, key_block, value_block, key_id):

        def full_block(inner_state):
            return absorb(inner_state, shaped[side], key_block, value_block, None, factor)

        def diagonal_block(inner_state):
            return absorb(inner_state, shaped[side], key_block, value_block, triangle, factor)

        def skipped(inner_state):
            return inner_state

        def not_below(inner_state):
            return lax.cond(key_id == query_ids[side], diagonal_block, skipped, inner_state)

        return lax.cond(key_id < query_ids[side], full_block, not_below, state)

    start_state = tuple(
        (
            (
                jnp.full((head_count, half_rows), NEG_BIG, jnp.float32),
                jnp.zeros((head_count, half_rows), jnp.float32),
                jnp.zeros((half_rows, head_count, head_width), jnp.float32),
            )
            for side in range(2)
        )
    )
    carry = start_state
    key_piece = lax.all_gather(k_soft, "seq", axis=0, tiled=True)
    value_piece = lax.all_gather(v_soft, "seq", axis=0, tiled=True)
    piece_rows = key_piece.shape[0]
    blocks = piece_rows // half_rows
    key_blocks = key_piece.reshape(blocks, half_rows, head_count, head_width)
    value_blocks = value_piece.reshape(blocks, half_rows, head_count, head_width)
    firsts = half_rows * jnp.arange(blocks, dtype=jnp.int32)

    def inner(state, block_item):
        key_block, value_block, first = block_item
        key_id = first // half_rows
        return (
            tuple(
                (block_pass(state[side], side, key_block, value_block, key_id) for side in range(2))
            ),
            None,
        )

    carry, _ = lax.scan(inner, carry, (key_blocks, value_blocks, firsts))
    halves = [
        (carry[side][2] / carry[side][1].T[:, :, None])
        .astype(jnp.bfloat16)
        .reshape(half_rows, head_count * head_width)
        for side in range(2)
    ]
    return jnp.concatenate(halves, axis=0)


def local(q_lin, k_lin, v_lin, log_decay, q_soft, k_soft, v_soft, wo_lin, wo_soft):
    head_width = q_lin.shape[1] // log_decay.shape[0]
    lin_out = lightning_heads(q_lin, k_lin, v_lin, log_decay)
    soft_out = softmax_heads(q_soft, k_soft, v_soft, head_width)
    lin_term = jnp.dot(lin_out, wo_lin, preferred_element_type=jnp.float32)
    soft_term = jnp.dot(soft_out, wo_soft, preferred_element_type=jnp.float32)
    lin_sum, soft_sum = (
        lax.psum_scatter(
            lin_term.astype(jnp.bfloat16).astype(jnp.float32).astype(jnp.bfloat16),
            "head",
            scatter_dimension=1,
            tiled=True,
        ).astype(jnp.float32),
        lax.psum_scatter(
            soft_term.astype(jnp.bfloat16).astype(jnp.float32).astype(jnp.bfloat16),
            "head",
            scatter_dimension=1,
            tiled=True,
        ).astype(jnp.float32),
    )
    return (lin_sum.astype(jnp.bfloat16), soft_sum.astype(jnp.bfloat16))


def solution(mesh):
    in_specs = (
        P("seq", "head"),
        P("seq", "head"),
        P("seq", "head"),
        P("head", "seq"),
        P("seq", "head"),
        P("seq", "head"),
        P("seq", "head"),
        P("head", None),
        P("head", None),
    )
    out_specs = (P("seq", "head"), P("seq", "head"))
    return jax.shard_map(local, mesh=mesh, in_specs=in_specs, out_specs=out_specs, check_vma=False)
```

profile of v0, /device:TPU:0, one launch (start us, length us, event | category | flops | bytes accessed | tf_op | source)
XLA Modules:
  0.0 389.1 jit_solution(17133437121583700277)
XLA Ops:
  9.3 1.0 copy.69
  10.4 1.8 convolution_convert_fusion.2
  13.8 1.2 dynamic-slice
  15.9 43.7 %all-reduce = bf16[32]{0:T(256)(128)(2,1)S(1)} all-reduce(bf16[32]{0:T(256)(128)(2,1)S(1)} %dynamic-update-slice), channel_id=2, replica_groups=mesh['seq'=16,'head'=2] {'seq'}, use_global_device_ids=true, to_apply=%add | all-reduce | flops 32 | bytes 128
  59.7 1.0 reshape.130
  60.7 1.1 convolution_multiply_fusion.4
  61.8 8.6 %all-gather.10.cloned.1.call-done = bf16[32,128,128]{2,1,0:T(8,128)(2,1)} async-done(((bf16[2,128,128]{2,1,0:T(8,128)(2,1)}), bf16[32,128,128]{2,1,0:T(8,128)(2,1)}) %all-gather.10.cloned.1.call-update) | async-done | bytes 1048592 | tf_op jit(solution)/shard_map/all_gather | solution.py:14
  70.5 15.6 %while.39 = (s32[]{:T(128)}, f32[2,128,128]{2,1,0:T(8,128)S(1)}, s32[]{:T(128)}, bf16[16,2]{1,0:T(8,128)(2,1)S(1)}, bf16[16,2,128,128]{3,2,1,0:T(8,128)(2,1)}, /*index=5*/s32[]{:T(128)}, s32[]{:T(128)}) while((s32[]{:T(128)}, f32[2,128,128]{2,1,0:T(8,128)S(1)}, s32[]{:T(128)}, bf16[16,2]{1,0:T(8,128)(2,1)S(1)}, ...), condition=%wide.region_3.4_spmd.clone, body=%wide.region_2.3_spmd.clone.sunk | while | flops 163846 | bytes 327813 | solution.py:31
  86.9 2.1 convolution_convert_fusion.1
  89.1 43.7 %all-gather.6.cloned.1.call-done = bf16[4096,256]{1,0:T(8,128)(2,1)} async-done(((bf16[256,256]{1,0:T(8,128)(2,1)}), bf16[4096,256]{1,0:T(8,128)(2,1)}) %all-gather.6.cloned.1.call-update) | async-done | bytes 2097168 | tf_op jit(solution)/shard_map/all_gather | solution.py:132
  132.8 4.0 %reshape.143 = bf16[32,128,2,128]{3,2,1,0:T(2,128)(2,1)} reshape(bf16[4096,256]{1,0:T(8,128)(2,1)} %all-gather.6.cloned.1.call-done) | data formatting | bytes 4194304 | tf_op jit(solution)/shard_map/reshape | solution.py:136
  136.8 58.2 %all-gather.8.cloned.1.call-done = bf16[4096,256]{1,0:T(8,128)(2,1)} async-done(((bf16[256,256]{1,0:T(8,128)(2,1)}), bf16[4096,256]{1,0:T(8,128)(2,1)}) %all-gather.8.cloned.1.call-update) | async-done | bytes 2097168 | tf_op jit(solution)/shard_map/all_gather | solution.py:133
  195.0 4.0 %reshape.144 = bf16[32,128,2,128]{3,2,1,0:T(2,128)(2,1)} reshape(bf16[4096,256]{1,0:T(8,128)(2,1)} %all-gather.8.cloned.1.call-done) | data formatting | bytes 4194304 | tf_op jit(solution)/shard_map/reshape | solution.py:137
  199.0 141.2 %while.38 = (s32[]{:T(128)}, f32[2,128]{1,0:T(2,128)S(1)}, f32[2,128]{1,0:T(2,128)S(1)}, f32[128,2,128]{2,0,1:T(8,128)S(1)}, f32[2,128]{1,0:T(2,128)S(1)}, /*ind...) while((s32[]{:T(128)}, f32[2,128]{1,0:T(2,128)S(1)}, ...), condition=%wide.region_23.24_spmd.clone.clone, body=%wide.region_6.23_spmd.clone.clone.sunk | while | flops 34162200 | bytes 2311003 | solution.py:150
  202.3 1.0 constant_dynamic-slice_fusion.3
  207.7 1.0 constant_dynamic-slice_fusion.3
  212.6 1.0 constant_dynamic-slice_fusion.3
  216.9 1.0 constant_dynamic-slice_fusion.3
  221.3 1.0 constant_dynamic-slice_fusion.3
  225.7 1.0 constant_dynamic-slice_fusion.3
  230.0 1.0 constant_dynamic-slice_fusion.3
  234.4 1.0 constant_dynamic-slice_fusion.3
  238.7 1.0 constant_dynamic-slice_fusion.3
  243.1 1.0 constant_dynamic-slice_fusion.3
  247.5 1.0 constant_dynamic-slice_fusion.3
  251.8 1.0 constant_dynamic-slice_fusion.3
  256.2 1.0 constant_dynamic-slice_fusion.3
  260.5 1.0 constant_dynamic-slice_fusion.3
  264.9 1.0 constant_dynamic-slice_fusion.3
  269.3 1.0 constant_dynamic-slice_fusion.3
  273.6 1.0 constant_dynamic-slice_fusion.3
  278.0 1.0 constant_dynamic-slice_fusion.3
  282.4 1.0 constant_dynamic-slice_fusion.3
  286.7 1.0 constant_dynamic-slice_fusion.3
  291.1 1.0 constant_dynamic-slice_fusion.3
  295.4 1.0 constant_dynamic-slice_fusion.3
  299.8 1.0 constant_dynamic-slice_fusion.3
  304.2 1.0 constant_dynamic-slice_fusion.3
  308.5 1.0 constant_dynamic-slice_fusion.3
  312.9 1.0 constant_dynamic-slice_fusion.3
  317.2 1.0 constant_dynamic-slice_fusion.3
  321.6 1.0 constant_dynamic-slice_fusion.3
  326.0 1.0 constant_dynamic-slice_fusion.3
  330.3 1.0 constant_dynamic-slice_fusion.3
  334.7 1.0 constant_dynamic-slice_fusion.3
  339.1 1.0 constant_dynamic-slice_fusion.3
  340.4 3.6 convolution_convert_fusion
  344.1 38.5 %reduce-scatter.5.cloned.1.call-done = bf16[256,2048]{1,0:T(8,128)(2,1)} async-done(((bf16[256,4096]{1,0:T(8,128)(2,1)}), bf16[256,2048]{1,0:T(8,128)(2,1)}) %reduce-scatter.5.cloned.1.call-update) | async-done | bytes 1048592 | tf_op jit(solution)/shard_map/reduce_scatter | solution.py:173
  (353 shorter events, 48.1 us)
Async XLA Ops:
  7.2 79.8 %copy-start = (bf16[256,4096]{1,0:T(8,128)(2,1)S(1)}, bf16[256,4096]{1,0:T(8,128)(2,1)}, u32[]{:S(2)}) copy-start(bf16[256,4096]{1,0:T(8,128)(2,1)} %param.28) | copy-start | bytes 6291460
  7.2 63.3 %all-gather.10.cloned.1.call-start = ((), (), s32[]{:S(2)}) async-start(), calls=%async_computation.6 | async-start | bytes 1114112 | tf_op jit(solution)/shard_map/all_gather | solution.py:14
  10.3 75.7 %copy-start.2 = (bf16[256,256]{1,0:T(8,128)(2,1)S(1)}, bf16[256,256]{1,0:T(8,128)(2,1)}, u32[]{:S(2)}) copy-start(bf16[256,256]{1,0:T(8,128)(2,1)} %param.21) | copy-start | bytes 393220
  12.2 120.6 %all-gather.6.cloned.1.call-start = ((), (), s32[]{:S(2)}) async-start(), calls=%async_computation.3 | async-start | bytes 2228224 | tf_op jit(solution)/shard_map/all_gather | solution.py:132
  13.0 73.4 %copy-start.1 = (bf16[256,256]{1,0:T(8,128)(2,1)S(1)}, bf16[256,256]{1,0:T(8,128)(2,1)}, u32[]{:S(2)}) copy-start(bf16[256,256]{1,0:T(8,128)(2,1)} %param.23) | copy-start | bytes 393220
  13.0 182.0 %all-gather.8.cloned.1.call-start = ((), (), s32[]{:S(2)}) async-start(), calls=%async_computation.4 | async-start | bytes 2228224 | tf_op jit(solution)/shard_map/all_gather | solution.py:133
  13.7 330.4 %reduce-scatter.3.cloned.1.call-start = ((), (), s32[]{:S(2)}) async-start(), calls=%async_computation.2 | async-start | bytes 3145728 | tf_op jit(solution)/shard_map/reduce_scatter | solution.py:167
  89.0 293.5 %reduce-scatter.5.cloned.1.call-start = ((), (), s32[]{:S(2)}) async-start(), calls=%async_computation.5 | async-start | bytes 3145728 | tf_op jit(solution)/shard_map/reduce_scatter | solution.py:173
Sparse Core Ops, SparseCore 0:
  12.3 58.0 all-gather.9
  73.2 59.5 all-gather.5
  135.6 59.3 all-gather.7
  197.6 8.2 reduce-scatter.2
  344.2 38.3 reduce-scatter.4
where the time goes:
time: 393 us; the launch traced here: 389 us
  waiting for transfers between devices  150 us (38%)
  loops' own time  89.1 us (23%)
  local copies, waits for them, and re-layouts  63.5 us (16%)
  blocking collectives  43.7 us (11%)
  other arithmetic  16.9 us (4%)
  between operations  14.6 us (4%)
  matrix products  10.7 us (3%)
    another operation x1, loops' own time, softmax_heads(): carry, _ = lax.scan(inner, carry, (key_blocks, value_blocks, firsts))  85.6 us
    all_gather x1, waiting for transfers between devices, softmax_heads(): value_piece = lax.all_gather(v_soft, 'seq', axis=0, tiled=True)  58.2 us
    dynamic_slice x128, local copies, waits for them, and re-layouts, softmax_heads(): carry, _ = lax.scan(inner, carry, (key_blocks, value_blocks, firsts))  50.6 us
    all_gather x1, waiting for transfers between devices, softmax_heads(): key_piece = lax.all_gather(k_soft, 'seq', axis=0, tiled=True)  43.7 us
    unnamed x1, blocking collectives  43.7 us
    reduce_scatter x1, waiting for transfers between devices, local(): lax.psum_scatter(soft_term.astype(jnp.bfloat16).astype(jnp.float32).astyp...  38.5 us
    select_n x16, other arithmetic, turn(): return jax.tree.map(lambda a, b: jnp.where(reached, a, b), new, before)  14.9 us
    all_gather x1, waiting for transfers between devices, prefix(): lax.all_gather(part.astype(kind), axis)  8.65 us
  transfers between devices with their start and end apart: 5, of which 4 were waited for; matrix products, arithmetic and copies ran while one was open for 22% of the time, Pallas kernels for 0%

commit v1 on v0

--- a/solution.py
+++ b/solution.py
@@ -129,8 +129,13 @@
         )
     )
     carry = start_state
-    key_piece = lax.all_gather(k_soft, "seq", axis=0, tiled=True)
-    value_piece = lax.all_gather(v_soft, "seq", axis=0, tiled=True)
+
+    def _play_series_all(xs, block_in):
+        next_value = jnp.concatenate([xs, block_in], axis=1)
+        near = lax.all_gather(next_value, "seq", axis=0, tiled=True)
+        return jnp.split(near, [xs.shape[1]], axis=1)
+
+    key_piece, value_piece = _play_series_all(k_soft, v_soft)
     piece_rows = key_piece.shape[0]
     blocks = piece_rows // half_rows
     key_blocks = key_piece.reshape(blocks, half_rows, head_count, head_width)

time: 393 us -> 355 us (0.903)
  waiting for transfers between devices: 150 us -> 107 us
  local copies, waits for them, and re-layouts: 63.5 us -> 68.2 us
    all_gather x2 -> x1, waiting for transfers between devices: 102 us -> 59.4 us  [_play_series_all(): near = lax.all_gather(next_value, 'seq', axis=0, tiled=True)]
    split x0 -> x1, local copies, waits for them, and re-layouts: none -> 4.47 us  [_play_series_all(): return jnp.split(near, [xs.shape[1]], axis=1)]
  transfers between devices with their start and end apart: 5 -> 4, of which waited for: 4 -> 3; matrix products, arithmetic and copies ran while one was open for 22% -> 26% of each run, Pallas kernels for 0% -> 0%
where the time goes in v1:
time: 355 us; the launch traced here: 351 us
  waiting for transfers between devices  107 us (30%)
  loops' own time  89 us (25%)
  local copies, waits for them, and re-layouts  68.2 us (19%)
  blocking collectives  43.8 us (12%)
  other arithmetic  18.6 us (5%)
  between operations  14.7 us (4%)
  matrix products  9.85 us (3%)
    another operation x1, loops' own time, softmax_heads(): carry, _ = lax.scan(inner, carry, (key_blocks, value_blocks, firsts))  85.5 us
    all_gather x1, waiting for transfers between devices, _play_series_all(): near = lax.all_gather(next_value, 'seq', axis=0, tiled=True)  59.4 us
    dynamic_slice x128, local copies, waits for them, and re-layouts, softmax_heads(): carry, _ = lax.scan(inner, carry, (key_blocks, value_blocks, firsts))  50.6 us
    unnamed x1, blocking collectives  43.8 us
    reduce_scatter x1, waiting for transfers between devices, local(): lax.psum_scatter(soft_term.astype(jnp.bfloat16).astype(jnp.float32).astyp...  38.3 us
    select_n x16, other arithmetic, turn(): return jax.tree.map(lambda a, b: jnp.where(reached, a, b), new, before)  14.9 us
    all_gather x1, waiting for transfers between devices, prefix(): lax.all_gather(part.astype(kind), axis)  9.04 us
  transfers between devices with their start and end apart: 4, of which 3 were waited for; matrix products, arithmetic and copies ran while one was open for 26% of the time, Pallas kernels for 0%

profile of v1, /device:TPU:0, one launch (start us, length us, event | category | flops | bytes accessed | tf_op | source)
XLA Modules:
  0.0 351.0 jit_solution(7655627925973001746)
XLA Ops:
  9.4 1.0 copy.69
  10.4 1.8 convolution_convert_fusion.2
  12.2 1.7 pad_maximum_fusion
  14.0 1.3 dynamic-slice
  16.3 43.8 %all-reduce = bf16[32]{0:T(256)(128)(2,1)S(1)} all-reduce(bf16[32]{0:T(256)(128)(2,1)S(1)} %dynamic-update-slice), channel_id=2, replica_groups=mesh['seq'=16,'head'=2] {'seq'}, use_global_device_ids=true, to_apply=%add | all-reduce | flops 32 | bytes 128
  60.2 1.0 reshape.130
  61.4 9.0 %all-gather.7.cloned.1.call-done = bf16[32,128,128]{2,1,0:T(8,128)(2,1)} async-done(((bf16[2,128,128]{2,1,0:T(8,128)(2,1)}), bf16[32,128,128]{2,1,0:T(8,128)(2,1)}) %all-gather.7.cloned.1.call-update) | async-done | bytes 1048592 | tf_op jit(solution)/shard_map/all_gather | solution.py:14
  70.5 15.6 %while.39 = (s32[]{:T(128)}, f32[2,128,128]{2,1,0:T(8,128)S(1)}, s32[]{:T(128)}, bf16[16,2]{1,0:T(8,128)(2,1)S(1)}, bf16[16,2,128,128]{3,2,1,0:T(8,128)(2,1)}, /*index=5*/s32[]{:T(128)}, s32[]{:T(128)}) while((s32[]{:T(128)}, f32[2,128,128]{2,1,0:T(8,128)S(1)}, s32[]{:T(128)}, bf16[16,2]{1,0:T(8,128)(2,1)S(1)}, ...), condition=%wide.region_3.4_spmd.clone, body=%wide.region_2.3_spmd.clone.sunk | while | flops 163846 | bytes 327813 | solution.py:31
  86.9 2.1 convolution_convert_fusion.1
  89.1 59.4 %all-gather.5.cloned.1.call-done = bf16[4096,512]{1,0:T(8,128)(2,1)} async-done(((bf16[256,512]{1,0:T(8,128)(2,1)}), bf16[4096,512]{1,0:T(8,128)(2,1)}) %all-gather.5.cloned.1.call-update) | async-done | bytes 4194320 | tf_op jit(solution)/shard_map/all_gather | solution.py:135
  148.5 4.5 %fusion.58 = (bf16[4096,256]{1,0:T(8,128)(2,1)}, bf16[4096,256]{1,0:T(8,128)(2,1)}) fusion(bf16[4096,512]{1,0:T(8,128)(2,1)} %all-gather.5.cloned.1.call-done), kind=kLoop, calls=%fused_computation.100 | loop fusion | bytes 8388608 | tf_op jit(solution)/shard_map/split | solution.py:136
  152.9 4.1 %reshape.144 = bf16[32,128,2,128]{3,2,1,0:T(2,128)(2,1)} reshape(bf16[4096,256]{1,0:T(8,128)(2,1)} %get-tuple-element.613) | data formatting | bytes 4194304 | tf_op jit(solution)/shard_map/reshape | solution.py:142
  157.0 4.0 %reshape.143 = bf16[32,128,2,128]{3,2,1,0:T(2,128)(2,1)} reshape(bf16[4096,256]{1,0:T(8,128)(2,1)} %get-tuple-element.614) | data formatting | bytes 4194304 | tf_op jit(solution)/shard_map/reshape | solution.py:141
  161.1 141.1 %while.38 = (s32[]{:T(128)}, f32[2,128]{1,0:T(2,128)S(1)}, f32[2,128]{1,0:T(2,128)S(1)}, f32[128,2,128]{2,0,1:T(8,128)S(1)}, f32[2,128]{1,0:T(2,128)S(1)}, /*ind...) while((s32[]{:T(128)}, f32[2,128]{1,0:T(2,128)S(1)}, ...), condition=%wide.region_23.24_spmd.clone.clone, body=%wide.region_6.23_spmd.clone.clone.sunk | while | flops 34162200 | bytes 2311003 | solution.py:155
  164.3 1.0 constant_dynamic-slice_fusion.3
  169.7 1.0 constant_dynamic-slice_fusion.3
  174.6 1.0 constant_dynamic-slice_fusion.3
  179.0 1.0 constant_dynamic-slice_fusion.3
  183.3 1.0 constant_dynamic-slice_fusion.3
  187.7 1.0 constant_dynamic-slice_fusion.3
  192.1 1.0 constant_dynamic-slice_fusion.3
  196.4 1.0 constant_dynamic-slice_fusion.3
  200.8 1.0 constant_dynamic-slice_fusion.3
  205.1 1.0 constant_dynamic-slice_fusion.3
  209.5 1.0 constant_dynamic-slice_fusion.3
  213.9 1.0 constant_dynamic-slice_fusion.3
  218.2 1.0 constant_dynamic-slice_fusion.3
  222.6 1.0 constant_dynamic-slice_fusion.3
  226.9 1.0 constant_dynamic-slice_fusion.3
  231.3 1.0 constant_dynamic-slice_fusion.3
  235.7 1.0 constant_dynamic-slice_fusion.3
  240.0 1.0 constant_dynamic-slice_fusion.3
  244.4 1.0 constant_dynamic-slice_fusion.3
  248.8 1.0 constant_dynamic-slice_fusion.3
  253.1 1.0 constant_dynamic-slice_fusion.3
  257.5 1.0 constant_dynamic-slice_fusion.3
  261.8 1.0 constant_dynamic-slice_fusion.3
  266.2 1.0 constant_dynamic-slice_fusion.3
  270.6 1.0 constant_dynamic-slice_fusion.3
  274.9 1.0 constant_dynamic-slice_fusion.3
  279.3 1.0 constant_dynamic-slice_fusion.3
  283.7 1.0 constant_dynamic-slice_fusion.3
  288.0 1.0 constant_dynamic-slice_fusion.3
  292.4 1.0 constant_dynamic-slice_fusion.3
  296.7 1.0 constant_dynamic-slice_fusion.3
  301.1 1.0 constant_dynamic-slice_fusion.3
  302.5 3.7 %convolution_convert_fusion = bf16[256,4096]{1,0:T(8,128)(2,1)} fusion(bf16[256,4096]{1,0:T(8,128)(2,1)} %param.29, bf16[128,256]{0,1:T(8,128)(2,1)S(1)} %bitcast.150, bf16[128,256]{0,1:T(8,128)(2,1)S(1)} %bitcast.151), kind=kOutput, calls=%fused_computation.59 | convolution fusion | flops 538181632 | bytes 4325376 | tf_op jit(solution)/shard_map/dot_general | solution.py:170
  306.2 38.3 %reduce-scatter.5.cloned.1.call-done = bf16[256,2048]{1,0:T(8,128)(2,1)} async-done(((bf16[256,4096]{1,0:T(8,128)(2,1)}), bf16[256,2048]{1,0:T(8,128)(2,1)}) %reduce-scatter.5.cloned.1.call-update) | async-done | bytes 1048592 | tf_op jit(solution)/shard_map/reduce_scatter | solution.py:178
  (352 shorter events, 47.0 us)
Async XLA Ops:
  7.2 79.8 %copy-start = (bf16[256,4096]{1,0:T(8,128)(2,1)S(1)}, bf16[256,4096]{1,0:T(8,128)(2,1)}, u32[]{:S(2)}) copy-start(bf16[256,4096]{1,0:T(8,128)(2,1)} %param.28) | copy-start | bytes 6291460
  7.2 54.0 %copy-start.2 = (bf16[256,256]{1,0:T(8,128)(2,1)S(1)}, bf16[256,256]{1,0:T(8,128)(2,1)}, u32[]{:S(2)}) copy-start(bf16[256,256]{1,0:T(8,128)(2,1)} %param.21) | copy-start | bytes 393220
  7.2 63.3 %all-gather.7.cloned.1.call-start = ((), (), s32[]{:S(2)}) async-start(), calls=%async_computation.5 | async-start | bytes 1114112 | tf_op jit(solution)/shard_map/all_gather | solution.py:14
  12.2 136.3 %all-gather.5.cloned.1.call-start = ((), (), s32[]{:S(2)}) async-start(), calls=%async_computation.3 | async-start | bytes 4456448 | tf_op jit(solution)/shard_map/all_gather | solution.py:135
  13.9 72.5 %copy-start.1 = (bf16[256,256]{1,0:T(8,128)(2,1)S(1)}, bf16[256,256]{1,0:T(8,128)(2,1)}, u32[]{:S(2)}) copy-start(bf16[256,256]{1,0:T(8,128)(2,1)} %param.23) | copy-start | bytes 393220
  14.0 292.2 %reduce-scatter.3.cloned.1.call-start = ((), (), s32[]{:S(2)}) async-start(), calls=%async_computation.2 | async-start | bytes 3145728 | tf_op jit(solution)/shard_map/reduce_scatter | solution.py:172
  89.0 255.5 %reduce-scatter.5.cloned.1.call-start = ((), (), s32[]{:S(2)}) async-start(), calls=%async_computation.4 | async-start | bytes 3145728 | tf_op jit(solution)/shard_map/reduce_scatter | solution.py:178
Sparse Core Ops, SparseCore 0:
  12.3 58.1 all-gather.6
  73.8 74.6 all-gather.4
  151.3 8.2 reduce-scatter.2
  306.3 38.1 reduce-scatter.4
